TPU v7x, 128 devices: a whole 4x4x4 slice. The times are simulated.
128 devices in a mesh: fsdp: 128 (over y, x, z, core).
Axes of the slice: x: 4, y: 4, z: 4, core: 2. Of those that a mesh axis runs over, the one named last changes fastest.
Arguments:
- tokens: bfloat16 [32768, 1024], P('fsdp'), may hold values from -6 to 6
- sequence_lengths: int32 [128, 4], P('fsdp'), may hold values from 0 to 256, as said below
- expert_index: int32 [32768, 8], P('fsdp'), may hold values from 0 to 11, all different within a row; in each aligned block of 256 rows (0 to 255, 256 to 511, ...) at most 203 rows name the same one
- cotangent: bfloat16 [32768, 1024], P('fsdp'), may hold values from -24 to 24
- query_weight: bfloat16 [1024, 1024], P('fsdp'), may hold values from -0.25 to 0.25
- key_weight: bfloat16 [1024, 512], P('fsdp'), may hold values from -0.25 to 0.25
- value_weight: bfloat16 [1024, 512], P('fsdp'), may hold values from -0.1875 to 0.1875
- output_weight: bfloat16 [1024, 1024], P('fsdp'), may hold values from -0.75 to 0.75
- attention_gain: bfloat16 [1024], P('fsdp'), may hold values from 0.25 to 1.75
- router_weight: bfloat16 [1024, 12], P('fsdp'), may hold values from -0.09375 to 0.09375
- mixture_gain: bfloat16 [1024], P('fsdp'), may hold values from 0.25 to 1.75
- gate_weight: bfloat16 [12, 1024, 512], P(None, 'fsdp'), may hold values from -0.1875 to 0.1875
- up_weight: bfloat16 [12, 1024, 512], P(None, 'fsdp'), may hold values from -0.1875 to 0.1875
- down_weight: bfloat16 [12, 512, 1024], P(None, 'fsdp'), may hold values from -0.75 to 0.75
Outputs:
- layer_out: bfloat16 [32768, 1024], P('fsdp')
- grad_tokens: bfloat16 [32768, 1024], P('fsdp')
- query_grad: float32 [1024, 1024], P('fsdp')
- key_grad: float32 [1024, 512], P('fsdp')
- value_grad: float32 [1024, 512], P('fsdp')
- output_grad: float32 [1024, 1024], P('fsdp')
- attention_gain_grad: float32 [1024], P('fsdp')
- router_grad: float32 [1024, 12], P('fsdp')
- mixture_gain_grad: float32 [1024], P('fsdp')
- gate_grad: float32 [12, 1024, 512], P(None, 'fsdp')
- up_grad: float32 [12, 1024, 512], P(None, 'fsdp')
- down_grad: float32 [12, 512, 1024], P(None, 'fsdp')
Inputs may be any that keep to these rules, and one draw needn't show every extreme that they name: `sequence_lengths`: row b lists the sequences of block b in order from its first row; they sum to at most 256, and in every draw some block holds a single sequence of 256 rows. `expert_index`: each row names 8 different experts. No expert is named by more than 203 rows of one block of 256 rows, a bound that some block reaches.
All inputs are finite; a program needn't handle non-finite values.
Results may differ from a plain program's by a relative error of at most 0.015.
The roundings to bfloat16 on the way count: a program that leaves them out, or rounds other values in their place, can miss the bound.
Values may be sent and summed in bfloat16 or wider, within the bound.
No kernel may reach another device: no remote copies, remote signals or barrier semaphores. Data moves between devices by JAX's collectives and lax.ppermute only.
A program may use at most 384 MiB of HBM per device.

v0:
```python
import math

import jax
import jax.numpy as jnp
from jax import lax
from jax.sharding import PartitionSpec as P

D = 1024
HEADS = 16
KV_HEADS = 8
HEAD_DIM = 64
EXPERTS = 12
TOP = 8
SEQ_DEV = 4
TOK_DEV = 256
CAP = 203


epsilon = 1e-06
rope_base = 10000.0


def sent_together(arrays, axis, dim, along):
    columns = [a.reshape(*a.shape[:along], -1) for a in arrays]
    both = jnp.concatenate(columns, axis=along)
    whole, at, done = (lax.all_gather(both, axis, axis=dim, tiled=True), 0, [])
    for a, column in zip(arrays, columns):
        piece = whole[..., at : at + column.shape[along]]
        done.append(piece.reshape(*piece.shape[:along], *a.shape[along:]))
        at += column.shape[along]
    return tuple(done)


def in_one_piece(arrays, axis, dim, along):
    ends, at = ([], 0)
    for a in arrays[:-1]:
        at += a.shape[along]
        ends.append(at)
    both = jnp.concatenate(arrays, axis=along)
    return tuple(jnp.split(lax.all_gather(both, axis, axis=dim, tiled=True), ends, axis=along))


def cut_along(value, dim, size):
    dims = value.shape
    parts = value.reshape(*dims[:dim], size, dims[dim] // size, *dims[dim + 1 :])
    return jnp.moveaxis(parts, dim, 0)


def sum_packed(arrays, axis, dims):
    size = lax.axis_size(axis)
    parts = [cut_along(a, dim, size) for a, dim in zip(arrays, dims)]
    lines = jnp.concatenate([b.reshape(size, -1) for b in parts], axis=1)
    span = max(16, -(-lines.shape[1] // 1024) * 8)
    lines = jnp.pad(lines, ((0, 0), (0, span * 128 - lines.shape[1]))).reshape(-1, 128)
    ravelled, at, done = (lax.psum_scatter(lines, axis, tiled=True).reshape(-1), 0, [])
    for b in parts:
        part = b[0]
        done.append(ravelled[at : at + part.size].reshape(part.shape))
        at += part.size
    return tuple(done)


def rms_scale(activations):
    return lax.rsqrt(jnp.mean(activations * activations, axis=1, keepdims=True) + epsilon)


def seq_layout(lengths):
    ends_at = jnp.cumsum(lengths)
    starts_at = ends_at - lengths
    slot_index = jnp.arange(TOK_DEV, dtype=jnp.int32)
    segment = jnp.sum((slot_index[:, None] >= ends_at[None, :]).astype(jnp.int32), axis=1)
    owners = segment[:, None] == jnp.arange(SEQ_DEV, dtype=jnp.int32)[None, :]
    begins = jnp.sum(jnp.where(owners, starts_at[None, :], 0), axis=1)
    return (segment, slot_index - begins, segment < SEQ_DEV)


def rope_tables(position):
    half_size = HEAD_DIM // 2
    frequency = rope_base ** (-2.0 * jnp.arange(half_size, dtype=jnp.float32) / HEAD_DIM)
    angles = position.astype(jnp.float32)[:, None] * frequency[None, :]
    return (jnp.cos(angles)[:, None, :], jnp.sin(angles)[:, None, :])


def rotate(operand, cosine, sine_part):
    half_size = operand.shape[-1] // 2
    first_half = operand[..., :half_size]
    second_half = operand[..., half_size:]
    return jnp.concatenate(
        [
            first_half * cosine - second_half * sine_part,
            second_half * cosine + first_half * sine_part,
        ],
        axis=-1,
    )


def norm_backward(activations, inv_rms, gain_values, grad_normed):
    grad_gain = jnp.sum(grad_normed * activations * inv_rms, axis=0)
    scaled_grad = grad_normed * gain_values
    grad_input = inv_rms * scaled_grad - activations * inv_rms**3 * jnp.mean(
        scaled_grad * activations, axis=1, keepdims=True
    )
    return (grad_input, grad_gain)


def shards(
    tokens,
    sequence_lengths,
    expert_index,
    cotangent,
    query_weight,
    key_weight,
    value_weight,
    output_weight,
    attention_gain,
    router_weight,
    mixture_gain,
    gate_weight,
    up_weight,
    down_weight,
):
    bfloat = jnp.bfloat16
    single = jnp.float32
    group_size = HEADS // KV_HEADS
    score_scale = 1.0 / math.sqrt(HEAD_DIM)
    attention_full = sent_together(
        (query_weight, key_weight, value_weight, output_weight, attention_gain), "fsdp", 0, 1
    )
    mixture_full = (
        *sent_together((router_weight, mixture_gain), "fsdp", 0, 1),
        *in_one_piece((gate_weight, up_weight), "fsdp", 1, 0),
        lax.all_gather(down_weight, "fsdp", axis=1, tiled=True),
    )
    query_full, key_full, value_full, output_full, attn_gain_full = attention_full
    router_full, mix_gain_full, gate_full, up_full, down_full = mixture_full
    segment, position, valid_slot = seq_layout(sequence_lengths[0])
    slot_index = jnp.arange(TOK_DEV, dtype=jnp.int32)
    valid_rows = valid_slot.astype(single)[:, None]
    token_values = tokens.astype(single)
    inv_first = rms_scale(token_values)
    normed_first = (token_values * inv_first * attn_gain_full.astype(single)).astype(bfloat)
    query_raw = jnp.dot(normed_first, query_full, preferred_element_type=single)
    key_raw = jnp.dot(normed_first, key_full, preferred_element_type=single)
    value_rows = (
        jnp.dot(normed_first, value_full, preferred_element_type=single)
        .astype(bfloat)
        .reshape(TOK_DEV, KV_HEADS, HEAD_DIM)
    )
    cosine, sine_part = rope_tables(position)
    query_rot = (
        rotate(query_raw.reshape(TOK_DEV, HEADS, HEAD_DIM), cosine, sine_part)
        .astype(bfloat)
        .reshape(TOK_DEV, KV_HEADS, group_size, HEAD_DIM)
    )
    key_rot = rotate(key_raw.reshape(TOK_DEV, KV_HEADS, HEAD_DIM), cosine, sine_part).astype(bfloat)
    allowed = (segment[:, None] == segment[None, :]) & (slot_index[None, :] <= slot_index[:, None])

    def scores_of(queries_in, keys_in):
        raw_scores = (
            jnp.einsum("tngd,snd->ngts", queries_in, keys_in, preferred_element_type=single)
            * score_scale
        )
        return jnp.where(allowed[None, None], raw_scores, -1e30)

    masked = scores_of(query_rot, key_rot)
    row_max = jnp.max(masked, axis=-1, keepdims=True)
    exp_terms = jnp.exp(masked - row_max)
    row_total = jnp.sum(exp_terms, axis=-1, keepdims=True)
    probability = exp_terms / row_total
    log_total = row_max + jnp.log(row_total)
    mixed_heads = jnp.einsum(
        "ngts,snd->tngd", probability.astype(bfloat), value_rows, preferred_element_type=single
    )
    attended = mixed_heads.reshape(TOK_DEV, HEADS * HEAD_DIM).astype(bfloat)
    branch = jnp.dot(attended, output_full, preferred_element_type=single)
    hidden = token_values + valid_rows * branch
    inv_second = rms_scale(hidden)
    normed_second = (hidden * inv_second * mix_gain_full.astype(single)).astype(bfloat)
    logits = jnp.dot(normed_second, router_full, preferred_element_type=single)
    pick_mask = expert_index[:, :, None] == jnp.arange(EXPERTS, dtype=jnp.int32)[None, None, :]
    picked = jnp.sum(jnp.where(pick_mask, logits[:, None, :], 0.0), axis=-1)
    gate_values = jax.nn.softmax(picked, axis=-1)
    pair_count = TOK_DEV * TOP
    flat_expert = expert_index.reshape(pair_count)
    onehot_pairs = (flat_expert[:, None] == jnp.arange(EXPERTS, dtype=jnp.int32)[None, :]).astype(
        jnp.int32
    )
    running = jnp.cumsum(onehot_pairs, axis=0)
    slot_rank = jnp.sum(running * onehot_pairs, axis=1) - 1
    destination = flat_expert * CAP + slot_rank
    pair_ids = jnp.arange(pair_count, dtype=jnp.int32)
    slot_source = jnp.full((EXPERTS * CAP,), pair_count, jnp.int32).at[destination].set(pair_ids)
    filled = slot_source < pair_count
    source_token = jnp.where(filled, slot_source // TOP, TOK_DEV)
    padded_normed = jnp.concatenate([normed_second, jnp.zeros((1, D), bfloat)], axis=0)
    expert_rows = padded_normed[source_token].reshape(EXPERTS, CAP, D)
    gate_act = jnp.einsum("ecd,edf->ecf", expert_rows, gate_full, preferred_element_type=single)
    up_act = jnp.einsum("ecd,edf->ecf", expert_rows, up_full, preferred_element_type=single)
    inner_act = (jax.nn.silu(gate_act) * up_act).astype(bfloat)
    expert_out = jnp.einsum(
        "ecf,efd->ecd", inner_act, down_full, preferred_element_type=single
    ).reshape(EXPERTS * CAP, D)
    pair_out = expert_out[destination].reshape(TOK_DEV, TOP, D)
    mixture = jnp.sum(gate_values[:, :, None] * pair_out, axis=1)
    layer_out = (hidden + valid_rows * mixture).astype(bfloat)
    grad_out = cotangent.astype(single)
    router_back, mix_gain_back, gate_back, up_back, down_back = mixture_full
    grad_mixture = valid_rows * grad_out
    grad_gates = jnp.sum(grad_mixture[:, None, :] * pair_out, axis=-1)
    grad_pairs = (
        (gate_values[:, :, None] * grad_mixture[:, None, :]).astype(bfloat).reshape(pair_count, D)
    )
    padded_grad = jnp.concatenate([grad_pairs, jnp.zeros((1, D), bfloat)], axis=0)
    grad_expert_out = padded_grad[slot_source].reshape(EXPERTS, CAP, D)
    grad_inner = jnp.einsum(
        "ecd,efd->ecf", grad_expert_out, down_back, preferred_element_type=single
    )
    sigmoid_gate = jax.nn.sigmoid(gate_act)
    silu_gate = gate_act * sigmoid_gate
    grad_gate_act = (
        grad_inner * up_act * sigmoid_gate * (1.0 + gate_act * (1.0 - sigmoid_gate))
    ).astype(bfloat)
    grad_up_act = (grad_inner * silu_gate).astype(bfloat)
    grad_rows = jnp.einsum(
        "ecf,edf->ecd", grad_gate_act, gate_back, preferred_element_type=single
    ) + jnp.einsum("ecf,edf->ecd", grad_up_act, up_back, preferred_element_type=single)
    grad_from_experts = jnp.sum(
        grad_rows.reshape(EXPERTS * CAP, D)[destination].reshape(TOK_DEV, TOP, D), axis=1
    )
    gate_centered = jnp.sum(gate_values * grad_gates, axis=1, keepdims=True)
    grad_picked = gate_values * (grad_gates - gate_centered)
    grad_logits = jnp.sum(jnp.where(pick_mask, grad_picked[:, :, None], 0.0), axis=1).astype(bfloat)
    router_grad = jnp.dot(normed_second.T, grad_logits, preferred_element_type=single)
    grad_normed_second = grad_from_experts + jnp.dot(
        grad_logits, router_back.T, preferred_element_type=single
    )
    grad_hidden_norm, mixture_gain_grad = norm_backward(
        hidden, inv_second, mix_gain_back.astype(single), grad_normed_second
    )
    down_grad = jnp.einsum(
        "ecf,ecd->efd", inner_act, grad_expert_out, preferred_element_type=single
    )
    gate_grad = jnp.einsum(
        "ecd,ecf->edf", expert_rows, grad_gate_act, preferred_element_type=single
    )
    up_grad = jnp.einsum("ecd,ecf->edf", expert_rows, grad_up_act, preferred_element_type=single)
    mixture_grads = (
        lax.psum_scatter(router_grad, "fsdp", scatter_dimension=0, tiled=True),
        lax.psum_scatter(mixture_gain_grad, "fsdp", scatter_dimension=0, tiled=True),
        lax.psum_scatter(gate_grad, "fsdp", scatter_dimension=1, tiled=True),
        lax.psum_scatter(up_grad, "fsdp", scatter_dimension=1, tiled=True),
        lax.psum_scatter(down_grad, "fsdp", scatter_dimension=1, tiled=True),
    )
    router_owned, gain_owned, gate_owned, up_owned, down_owned = mixture_grads
    grad_hidden = grad_out + grad_hidden_norm
    query_back, key_back, value_back, output_back, attn_gain_back = attention_full
    grad_branch = (valid_rows * grad_hidden).astype(bfloat)
    output_grad = jnp.dot(attended.T, grad_branch, preferred_element_type=single)
    grad_attended = (
        jnp.dot(grad_branch, output_back.T, preferred_element_type=single)
        .astype(bfloat)
        .reshape(TOK_DEV, KV_HEADS, group_size, HEAD_DIM)
    )
    recomputed = jnp.exp(scores_of(query_rot, key_rot) - log_total)
    grad_probability = jnp.einsum(
        "tngd,snd->ngts", grad_attended, value_rows, preferred_element_type=single
    )
    grad_values = (
        jnp.einsum(
            "ngts,tngd->snd",
            recomputed.astype(bfloat),
            grad_attended,
            preferred_element_type=single,
        )
        .astype(bfloat)
        .reshape(TOK_DEV, KV_HEADS * HEAD_DIM)
    )
    row_dot = jnp.sum(recomputed * grad_probability, axis=-1, keepdims=True)
    grad_scores = (recomputed * (grad_probability - row_dot)).astype(bfloat)
    grad_query_rot = (
        jnp.einsum("ngts,snd->tngd", grad_scores, key_rot, preferred_element_type=single)
        * score_scale
    )
    grad_key_rot = (
        jnp.einsum("ngts,tngd->snd", grad_scores, query_rot, preferred_element_type=single)
        * score_scale
    )
    grad_query = (
        rotate(grad_query_rot.reshape(TOK_DEV, HEADS, HEAD_DIM), cosine, -sine_part)
        .astype(bfloat)
        .reshape(TOK_DEV, HEADS * HEAD_DIM)
    )
    grad_key = (
        rotate(grad_key_rot, cosine, -sine_part)
        .astype(bfloat)
        .reshape(TOK_DEV, KV_HEADS * HEAD_DIM)
    )
    query_grad = jnp.dot(normed_first.T, grad_query, preferred_element_type=single)
    key_grad = jnp.dot(normed_first.T, grad_key, preferred_element_type=single)
    value_grad = jnp.dot(normed_first.T, grad_values, preferred_element_type=single)
    grad_normed_first = (
        jnp.dot(grad_query, query_back.T, preferred_element_type=single)
        + jnp.dot(grad_key, key_back.T, preferred_element_type=single)
        + jnp.dot(grad_values, value_back.T, preferred_element_type=single)
    )
    grad_tokens_norm, attention_gain_grad = norm_backward(
        token_values, inv_first, attn_gain_back.astype(single), grad_normed_first
    )
    attention_grads = sum_packed(
        (query_grad, key_grad, value_grad, output_grad, attention_gain_grad),
        "fsdp",
        (0, 0, 0, 0, 0),
    )
    grad_tokens = (grad_hidden + grad_tokens_norm).astype(bfloat)
    return (
        layer_out,
        grad_tokens,
        attention_grads[0],
        attention_grads[1],
        attention_grads[2],
        attention_grads[3],
        attention_grads[4],
        router_owned,
        gain_owned,
        gate_owned,
        up_owned,
        down_owned,
    )


def solution(mesh):
    placed = (
        P("fsdp", None),
        P("fsdp", None),
        P("fsdp", None),
        P("fsdp", None),
        P("fsdp", None),
        P("fsdp", None),
        P("fsdp", None),
        P("fsdp", None),
        P("fsdp"),
        P("fsdp", None),
        P("fsdp"),
        P(None, "fsdp", None),
        P(None, "fsdp", None),
        P(None, "fsdp", None),
    )
    return jax.shard_map(
        shards,
        mesh=mesh,
        in_specs=placed,
        out_specs=(
            P("fsdp", None),
            P("fsdp", None),
            P("fsdp", None),
            P("fsdp", None),
            P("fsdp", None),
            P("fsdp", None),
            P("fsdp"),
            P("fsdp", None),
            P("fsdp"),
            P(None, "fsdp", None),
            P(None, "fsdp", None),
            P(None, "fsdp", None),
        ),
        check_vma=False,
    )
```

profile of v0, /device:TPU:0, one launch (start us, length us, event | category | flops | bytes accessed | tf_op | source)
XLA Modules:
  0.0 1322.7 jit_solution(938302408891625070)
XLA Ops:
  31.6 37.5 %all_gather.13 = bf16[1024,13]{1,0:T(8,128)(2,1)S(1)} all-gather(bf16[8,13]{1,0:T(8,128)(2,1)S(1)} %pad_maximum_fusion.6), channel_id=1, replica_groups=mesh['fsdp'=128] {'fsdp'}, dimensions={0}, use_global_device_ids=true | all-gather | bytes 26832 | tf_op jit(solution)/shard_map/all_gather | solution.py:26
  102.1 14.8 %gather_fusion.2 = bf16[2436,1024]{1,0:T(8,128)(2,1)} fusion(bf16[2049,1024]{1,0:T(8,128)(2,1)} %concatenate.47, s32[3072]{0:T(1024)S(1)} %get-tuple-element.56), kind=kCustom, calls=%fused_computation.2 | custom fusion | bytes 9987600 | tf_op jit(solution)/shard_map/gather | solution.py:214
  122.2 8.8 gather_fusion
  136.4 27.9 %all-gather.8.cloned.1.call-done = bf16[12,512,1024]{2,0,1:T(8,128)(2,1)} async-done(((bf16[12,4,1024]{2,0,1:T(8,128)(2,1)}), bf16[12,512,1024]{2,0,1:T(8,128)(2,1)}) %all-gather.8.cloned.1.call-update) | async-done | bytes 12582928 | tf_op jit(solution)/shard_map/all_gather | solution.py:132
  164.3 23.7 %fusion.8 = f32[12,203,512]{2,1,0:T(8,128)} fusion(bf16[12,203,1024]{2,1,0:T(8,128)(2,1)} %reshape.479, bf16[12,512,1024]{2,0,1:T(8,128)(2,1)} %all-gather.8.cloned.1.call-done), kind=kOutput, calls=%fused_computation.13 | convolution fusion | flops 2554331136 | bytes 22560768 | tf_op jit(solution)/shard_map/ecd,efd->ecf/dot_general | solution.py:215
  188.0 87.1 %all-gather.6.cloned.1.call-done = bf16[24,1024,512]{2,1,0:T(8,128)(2,1)} async-done(((bf16[24,8,512]{2,1,0:T(8,128)(2,1)}), bf16[24,1024,512]{2,1,0:T(8,128)(2,1)}) %all-gather.6.cloned.1.call-update) | async-done | bytes 25165840 | tf_op jit(solution)/shard_map/all_gather | solution.py:40
  275.1 11.3 fusion.2
  286.3 12.6 multiply_convert_fusion.1
  298.9 25.0 %fusion.10 = f32[12,203,1024]{2,1,0:T(8,128)} fusion(bf16[12,203,512]{2,1,0:T(8,128)(2,1)} %get-tuple-element.28, bf16[12,512,1024]{2,0,1:T(8,128)(2,1)} %all-gather.8.cloned.1.call-done), kind=kOutput, calls=%fused_computation.15 | convolution fusion | flops 2554331136 | bytes 25055232 | tf_op jit(solution)/shard_map/ecf,efd->ecd/dot_general | solution.py:200
  323.9 10.6 reshape.477
  334.5 15.7 %gather_fusion.1 = f32[2048,1024]{1,0:T(8,128)} fusion(f32[2436,1024]{1,0:T(8,128)} %reshape.477, s32[2048]{0:T(1024)S(1)} %copy-done.45), kind=kCustom, calls=%fused_computation.1 | custom fusion | bytes 16785408 | tf_op jit(solution)/shard_map/gather | solution.py:203
  356.9 13.3 %fusion = f32[12,203,1024]{2,1,0:T(8,128)} fusion(bf16[12,203,512]{2,1,0:T(8,128)(2,1)} %get-tuple-element.27, bf16[24,1024,512]{2,1,0:T(8,128)(2,1)} %all-gather.6.cloned.1.call-done), kind=kOutput, calls=%fused_computation.5 | convolution fusion | flops 2554331136 | bytes 25116672 | tf_op jit(solution)/shard_map/ecf,edf->ecd/dot_general | solution.py:226
  370.2 15.3 %fusion.20 = f32[12,203,1024]{2,1,0:T(8,128)} fusion(f32[12,203,1024]{2,1,0:T(8,128)} %fusion, bf16[12,203,512]{2,1,0:T(8,128)(2,1)S(1)} %copy-done.3, bf16[24,1024,512]{2,1,0:T(8,128)(2,1)} %all-gather.6.cloned.1.call-done), kind=kOutput, calls=%fused_computation.39 | convolution fusion | flops 2556825600 | bytes 35278848 | tf_op jit(solution)/shard_map/ecf,edf->ecd/dot_general | solution.py:224
  385.5 11.0 reshape.480
  396.4 15.6 %gather_fusion.3 = f32[2048,1024]{1,0:T(8,128)} fusion(f32[2436,1024]{1,0:T(8,128)} %reshape.480, s32[2048]{0:T(1024)S(1)} %copy-done.45), kind=kCustom, calls=%fused_computation.3 | custom fusion | bytes 16785408 | tf_op jit(solution)/shard_map/gather | solution.py:228
  437.5 10.1 fusion.102
  490.9 10.7 pad.6
  501.6 12.1 reshape.486
  513.8 13.7 %fusion.100 = f32[12,1024,512]{2,1,0:T(8,128)} fusion(bf16[12,203,1024]{2,1,0:T(8,128)(2,1)} %reshape.476, bf16[12,203,512]{2,1,0:T(8,128)(2,1)S(1)} %copy-done.3), kind=kOutput, calls=%fused_computation.195 | convolution fusion | flops 2554331136 | bytes 32649216 | tf_op jit(solution)/shard_map/ecd,ecf->edf/dot_general | solution.py:243
  529.3 13.6 %fusion.101 = f32[12,1024,512]{2,1,0:T(8,128)} fusion(bf16[12,203,1024]{2,1,0:T(8,128)(2,1)} %reshape.476, bf16[12,203,512]{2,1,0:T(8,128)(2,1)S(1)} %copy-done.4), kind=kOutput, calls=%fused_computation.196 | convolution fusion | flops 2554331136 | bytes 32649216 | tf_op jit(solution)/shard_map/ecd,ecf->edf/dot_general | solution.py:246
  544.3 70.4 %all-reduce.7 = (f32[1024,12]{1,0:T(8,128)S(1)}, f32[1024]{0:T(1024)S(1)}) all-reduce(f32[1024,12]{1,0:T(8,128)S(1)} %fusion.103, f32[1024]{0:T(1024)S(1)} %get-tuple-element.14), channel_id=3, replica_groups=mesh['fsdp'=128] {'fsdp'}, use_global_device_ids=true, to_apply=%region_24.25.clone | all-reduce | flops 13312 | bytes 106496
  618.3 194.1 %all-reduce.11.cloned.1.call-done = (f32[25600,128]{1,0:T(8,128)}, f32[12,512,1024]{2,1,0:T(8,128)}) async-done(((f32[25600,128]{1,0:T(8,128)}, f32[12,512,1024]{2,1,0:T(8,128)}), (f32[25600,128]{1,0:T(8,128)}, f32[12,512,1024]{2,1,0:T(8,128)})) %all-reduce.11.cloned.1.call-update) | async-done | bytes 38273040
  819.6 245.1 %reduce-scatter.4.cloned.1.call-done = f32[12,8,512]{2,1,0:T(8,128)} async-done(((f32[12,1024,512]{2,1,0:T(8,128)}), f32[12,8,512]{2,1,0:T(8,128)}) %reduce-scatter.4.cloned.1.call-update) | async-done | bytes 196624 | tf_op jit(solution)/shard_map/reduce_scatter | solution.py:250
  1064.7 250.9 %reduce-scatter.6.cloned.1.call-done = f32[12,8,512]{2,1,0:T(8,128)} async-done(((f32[12,1024,512]{2,1,0:T(8,128)}), f32[12,8,512]{2,1,0:T(8,128)}) %reduce-scatter.6.cloned.1.call-update) | async-done | bytes 196624 | tf_op jit(solution)/shard_map/reduce_scatter | solution.py:251
  (255 shorter events, 156.7 us)
Async XLA Ops:
  7.2 76.7 %copy-start.6 = (bf16[256,1024]{1,0:T(8,128)(2,1)S(1)}, bf16[256,1024]{1,0:T(8,128)(2,1)}, u32[]{:S(2)}) copy-start(bf16[256,1024]{1,0:T(8,128)(2,1)} %param.14) | copy-start | bytes 1572868
  7.2 75.6 %all-gather.4.cloned.1.call-start = ((), (), s32[]{:S(2)}) async-start(), calls=%async_computation.2 | async-start | bytes 6604800 | tf_op jit(solution)/shard_map/all_gather | solution.py:26
  11.5 152.7 %all-gather.8.cloned.1.call-start = ((), (), s32[]{:S(2)}) async-start(), calls=%async_computation.4 | async-start | bytes 16908288 | tf_op jit(solution)/shard_map/all_gather | solution.py:132
  13.2 261.9 %all-gather.6.cloned.1.call-start = ((), (), s32[]{:S(2)}) async-start(), calls=%async_computation.3 | async-start | bytes 25362432 | tf_op jit(solution)/shard_map/all_gather | solution.py:40
  14.9 797.5 %all-reduce.11.cloned.1.call-start = ((), (), s32[]{:S(2)}) async-start(), calls=%async_computation.7 | async-start | bytes 76546048
  69.1 28.2 %copy-start.20 = (bf16[1024,13]{1,0:T(8,128)(2,1)}, bf16[1024,13]{1,0:T(8,128)(2,1)S(1)}, u32[]{:S(2)}) copy-start(bf16[1024,13]{1,0:T(8,128)(2,1)S(1)} %all_gather.13) | copy-start | bytes 79876
  70.2 26.6 %copy-start.46 = (f32[1024]{0:T(1024)}, f32[1024]{0:T(1024)S(1)}, u32[]{:S(2)}) copy-start(f32[1024]{0:T(1024)S(1)} %convert_reduce_fusion) | copy-start | bytes 12292
  71.5 22.0 %copy-start.54 = (f32[256]{0:T(256)}, f32[256]{0:T(256)S(1)}, u32[]{:S(2)}) copy-start(f32[256]{0:T(256)S(1)} %compare_convert_fusion) | copy-start | bytes 3076
  72.1 18.4 %copy-start.48 = (f32[256]{0:T(256)}, f32[256]{0:T(256)S(1)}, u32[]{:S(2)}) copy-start(f32[256]{0:T(256)S(1)} %get-tuple-element.45) | copy-start | bytes 3076
  73.6 16.9 %copy-start.31 = (f32[256,32]{0,1:T(8,128)}, f32[256,32]{0,1:T(8,128)S(1)}, u32[]{:S(2)}) copy-start(f32[256,32]{0,1:T(8,128)S(1)} %get-tuple-element.43) | copy-start | bytes 98308
  74.8 23.8 %copy-start.14 = (f32[256,1024]{1,0:T(8,128)}, f32[256,1024]{1,0:T(8,128)S(1)}, u32[]{:S(2)}) copy-start(f32[256,1024]{1,0:T(8,128)S(1)} %convert_multiply_fusion.5) | copy-start | bytes 3145732
  83.8 6.6 copy-start.40
  275.1 11.3 copy-start
  323.9 10.6 copy-start.45
  334.5 15.8 %copy-start.15 = (f32[256,1024]{1,0:T(8,128)S(1)}, f32[256,1024]{1,0:T(8,128)}, u32[]{:S(2)}) copy-start(f32[256,1024]{1,0:T(8,128)} %copy-done.14) | copy-start | bytes 3145732
  334.5 15.8 %copy-start.25 = (f32[256,8]{1,0:T(8,128)S(1)}, f32[256,8]{1,0:T(8,128)}, u32[]{:S(2)}) copy-start(f32[256,8]{1,0:T(8,128)} %copy-done.24) | copy-start | bytes 24580
  356.9 13.3 %copy-start.3 = (bf16[12,203,512]{2,1,0:T(8,128)(2,1)S(1)}, bf16[12,203,512]{2,1,0:T(8,128)(2,1)}, u32[]{:S(2)}) copy-start(bf16[12,203,512]{2,1,0:T(8,128)(2,1)} %get-tuple-element.26) | copy-start | bytes 7483396
  437.5 10.2 copy-start.7
  437.5 10.1 copy-start.41
  437.5 10.1 copy-start.49
  513.7 551.0 %reduce-scatter.4.cloned.1.call-start = ((), (), s32[]{:S(2)}) async-start(), calls=%async_computation.5 | async-start | bytes 25362432 | tf_op jit(solution)/shard_map/reduce_scatter | solution.py:250
  527.5 788.2 %reduce-scatter.6.cloned.1.call-start = ((), (), s32[]{:S(2)}) async-start(), calls=%async_computation.6 | async-start | bytes 25362432 | tf_op jit(solution)/shard_map/reduce_scatter | solution.py:251
  542.9 73.0 %copy-start.13 = (f32[256,1024]{1,0:T(8,128)S(1)}, f32[256,1024]{1,0:T(8,128)}, u32[]{:S(2)}) copy-start(f32[256,1024]{1,0:T(8,128)} %copy-done.11) | copy-start | bytes 3145732
  542.9 73.0 %copy-start.56 = (f32[256]{0:T(256)S(1)}, f32[256]{0:T(256)}, u32[]{:S(2)}) copy-start(f32[256]{0:T(256)} %get-tuple-element.44) | copy-start | bytes 3076
  (42 other events, 163.4 us)
Sparse Core Ops, SparseCore 0:
  11.6 71.0 all-gather.3
  86.5 77.7 all-gather.7
  167.7 107.3 all-gather.5
  513.8 298.5 all-reduce.10
  819.0 245.6 reduce-scatter.3
  1071.3 244.2 reduce-scatter.5
where the time goes:
time: 1330 us; the launch traced here: 1320 us
  waiting for transfers between devices  813 us (61%)
  matrix products  178 us (13%)
  local copies, waits for them, and re-layouts  172 us (13%)
  blocking collectives  108 us (8%)
  other arithmetic  36.7 us (3%)
  between operations  15.2 us (1%)
    reduce_scatter x1, waiting for transfers between devices, shards(): lax.psum_scatter(up_grad, 'fsdp', scatter_dimension=1, tiled=True)  251 us
    reduce_scatter x1, waiting for transfers between devices, shards(): lax.psum_scatter(gate_grad, 'fsdp', scatter_dimension=1, tiled=True)  245 us
    unnamed x7, waiting for transfers between devices  194 us
    all_gather x1, waiting for transfers between devices, in_one_piece(): lax.all_gather(both, axis, axis=dim, tiled=True)  87.1 us
    unnamed x1, blocking collectives  70.4 us
    all_gather x1, blocking collectives, sent_together(): whole, at, done = (lax.all_gather(both, axis, axis=dim, tiled=True), 0, [])  37.5 us
    all_gather x1, waiting for transfers between devices, shards(): lax.all_gather(down_weight, 'fsdp', axis=1, tiled=True)  27.9 us
  transfers between devices with their start and end apart: 6, of which 6 were waited for; matrix products, arithmetic and copies ran while one was open for 11% of the time, Pallas kernels for 0%

commit v1 on v0

v1 whole, which is shorter than its diff:
```python
import math

import jax
import jax.numpy as jnp
from jax import lax
from jax.sharding import Mesh, PartitionSpec as P

D = 1024
HEADS = 16
KV_HEADS = 8
HEAD_DIM = 64
EXPERTS = 12
TOP = 8
SEQ_DEV = 4
TOK_DEV = 256
FF = 512
ALL = ("y", "x", "z", "core")


epsilon = 1e-06
rope_base = 10000.0


def shift(v, axis, s):
    n = lax.axis_size(axis)
    return lax.ppermute(v, axis, [(i, (i + s) % n) for i in range(n)])


def add_low(*terms):
    return sum(a.astype(jnp.float32) for a in terms).astype(jnp.bfloat16)


def group_gather(v):
    half = v.shape[0] // 2
    above = shift(v, "z", 1)
    below = shift(v, "z", -1)
    far = jnp.concatenate([shift(above[:half], "z", 1), shift(below[half:], "z", -1)], axis=0)
    blocks = []
    for block in (v, below, far, above):
        blocks += [block, shift(block, "core", 1)]
    return blocks


def ring_sum(parts, axis):
    half = parts[2].shape[0] // 2
    front = shift(parts[2][:half], axis, 1)
    back = shift(parts[2][half:], axis, -1)
    ahead = jnp.concatenate([add_low(parts[1][:half], front), parts[1][half:]], axis=0)
    behind = jnp.concatenate([parts[3][:half], add_low(parts[3][half:], back)], axis=0)
    return sum(a.astype(jnp.float32) for a in (parts[0], shift(ahead, axis, 1), shift(behind, axis, -1)))


def direct_sum(parts, axis):
    terms = (parts[0], shift(parts[1], axis, 1), shift(parts[2], axis, 2), shift(parts[3], axis, -1))
    return sum(a.astype(jnp.float32) for a in terms)


def group_sum(blocks):
    other = [shift(b, "core", 1) for b in blocks[1::2]]
    return ring_sum([add_low(a, b) for a, b in zip(blocks[::2], other)], "z")


def axis_sum(v, axis, dim, how):
    me = lax.axis_index(axis)
    parts = [lax.dynamic_index_in_dim(v, (me + k) % 4, dim, keepdims=False) for k in range(4)]
    return how(parts, axis)


def torus_sum(v, order, axes, how=ring_sum):
    axes = list(axes)
    for i, axis in enumerate(order):
        v = axis_sum(v, axis, axes.index(axis), how)
        axes.remove(axis)
        if i < len(order) - 1:
            v = v.astype(jnp.bfloat16)
    return v


def group_exchange(v):
    z, c = lax.axis_index("z"), lax.axis_index("core")
    keep = lax.dynamic_index_in_dim(v, c, 1, keepdims=False)
    got = shift(lax.dynamic_index_in_dim(v, 1 - c, 1, keepdims=False), "core", 1)
    first = jnp.where(c == 0, keep, got)
    second = jnp.where(c == 0, got, keep)
    both = jnp.stack([first, second], axis=1)
    parts = [lax.dynamic_index_in_dim(both, (z + k) % 4, 0, keepdims=False) for k in range(4)]
    came = [parts[0]] + [shift(parts[k], "z", k) for k in (1, 2, 3)]
    line = jnp.stack([came[0], came[3], came[2], came[1]] * 2, axis=0)
    return lax.dynamic_slice_in_dim(line, (4 - z) % 4, 4, axis=0)


def column_order():
    column = lax.broadcasted_iota(jnp.int32, (FF, FF), 1)
    feature = lax.broadcasted_iota(jnp.int32, (FF, FF), 0)
    return feature == (column // 4 % 16) * 32 + (column // 64) * 4 + column % 4


def expert_lanes():
    lane = lax.broadcasted_iota(jnp.int32, (EXPERTS, EXPERTS * 64), 1) // 64
    return lane == lax.broadcasted_iota(jnp.int32, (EXPERTS, EXPERTS * 64), 0)


def rms_scale(activations):
    return lax.rsqrt(jnp.mean(activations * activations, axis=1, keepdims=True) + epsilon)


def seq_layout(lengths):
    ends_at = jnp.cumsum(lengths)
    starts_at = ends_at - lengths
    slot_index = jnp.arange(TOK_DEV, dtype=jnp.int32)
    segment = jnp.sum((slot_index[:, None] >= ends_at[None, :]).astype(jnp.int32), axis=1)
    owners = segment[:, None] == jnp.arange(SEQ_DEV, dtype=jnp.int32)[None, :]
    begins = jnp.sum(jnp.where(owners, starts_at[None, :], 0), axis=1)
    return (segment, slot_index - begins, segment < SEQ_DEV)


def rope_tables(position):
    half_size = HEAD_DIM // 2
    frequency = rope_base ** (-2.0 * jnp.arange(half_size, dtype=jnp.float32) / HEAD_DIM)
    angles = position.astype(jnp.float32)[:, None] * frequency[None, :]
    return (jnp.cos(angles)[:, None, :], jnp.sin(angles)[:, None, :])


def rotate(operand, cosine, sine_part):
    half_size = operand.shape[-1] // 2
    first_half = operand[..., :half_size]
    second_half = operand[..., half_size:]
    return jnp.concatenate(
        [
            first_half * cosine - second_half * sine_part,
            second_half * cosine + first_half * sine_part,
        ],
        axis=-1,
    )


def norm_backward(activations, inv_rms, gain_values, grad_normed):
    grad_gain = jnp.sum(grad_normed * activations * inv_rms, axis=0)
    scaled_grad = grad_normed * gain_values
    grad_input = inv_rms * scaled_grad - activations * inv_rms**3 * jnp.mean(
        scaled_grad * activations, axis=1, keepdims=True
    )
    return (grad_input, grad_gain)


def shards(
    tokens,
    sequence_lengths,
    expert_index,
    cotangent,
    query_weight,
    key_weight,
    value_weight,
    output_weight,
    attention_gain,
    router_weight,
    mixture_gain,
    gate_weight,
    up_weight,
    down_weight,
):
    bfloat = jnp.bfloat16
    single = jnp.float32
    group_size = HEADS // KV_HEADS
    score_scale = 1.0 / math.sqrt(HEAD_DIM)
    wide = EXPERTS * 64
    small = jnp.concatenate(
        [router_weight, attention_gain[:, None], mixture_gain[:, None], jnp.zeros((8, 114), bfloat)], axis=1
    )
    attention_full = lax.all_gather(
        jnp.concatenate([query_weight, key_weight, value_weight, output_weight, small], axis=1),
        ALL, axis=0, tiled=True,
    )
    qkv_full = attention_full[:, :2048]
    output_full = attention_full[:, 2048:3072]
    router_full = attention_full[:, 3072:3084]
    gains = attention_full[:, 3084:3086].astype(single)
    attn_gain_full, mix_gain_full = gains[:, 0], gains[:, 1]
    order = column_order().astype(bfloat)
    gate_up = jnp.concatenate([gate_weight, up_weight], axis=0).reshape(24 * 8, FF)
    gate_up = jnp.dot(gate_up, order, preferred_element_type=single).astype(bfloat)
    gate_up = gate_up.reshape(24, 8, 8, 64).transpose(2, 1, 0, 3).reshape(4, 2, 8, 2 * wide)
    gate_up = group_exchange(gate_up).reshape(64, 2 * wide)
    gate_up_full = lax.all_gather(gate_up, ("y", "x"), axis=0, tiled=True)
    down_full = lax.all_gather(down_weight.reshape(48, D), ("y", "x"), axis=0, tiled=True)
    down_full = down_full.reshape(16, 12, 4, D).transpose(1, 0, 2, 3).reshape(wide, D)

    segment, position, valid_slot = seq_layout(sequence_lengths[0])
    slot_index = jnp.arange(TOK_DEV, dtype=jnp.int32)
    valid_rows = valid_slot.astype(single)[:, None]
    pick = jnp.any(
        expert_index[:, :, None] == jnp.arange(EXPERTS, dtype=jnp.int32)[None, None, :], axis=1
    ).astype(bfloat)
    grad_out = cotangent.astype(single)
    early = jnp.concatenate(
        [cotangent * valid_rows.astype(bfloat), pick, jnp.zeros((TOK_DEV, 116), bfloat)], axis=1
    )
    early = jnp.concatenate(group_gather(early), axis=0)
    grad_mixture = early[:, :D]
    pick_all = early[:, D : D + EXPERTS] > 0

    token_values = tokens.astype(single)
    inv_first = rms_scale(token_values)
    normed_first = (token_values * inv_first * attn_gain_full).astype(bfloat)
    qkv = jnp.dot(normed_first, qkv_full, preferred_element_type=single)
    query_raw, key_raw = qkv[:, :1024], qkv[:, 1024:1536]
    value_rows = qkv[:, 1536:].astype(bfloat).reshape(TOK_DEV, KV_HEADS, HEAD_DIM)
    cosine, sine_part = rope_tables(position)
    query_rot = (
        rotate(query_raw.reshape(TOK_DEV, HEADS, HEAD_DIM), cosine, sine_part)
        .astype(bfloat)
        .reshape(TOK_DEV, KV_HEADS, group_size, HEAD_DIM)
    )
    key_rot = rotate(key_raw.reshape(TOK_DEV, KV_HEADS, HEAD_DIM), cosine, sine_part).astype(bfloat)
    allowed = (segment[:, None] == segment[None, :]) & (slot_index[None, :] <= slot_index[:, None])

    raw_scores = jnp.einsum("tngd,snd->ngts", query_rot, key_rot, preferred_element_type=single)
    masked = jnp.where(allowed[None, None], raw_scores * score_scale, -1e30)
    row_max = jnp.max(masked, axis=-1, keepdims=True)
    exp_terms = jnp.exp(masked - row_max)
    probability = exp_terms / jnp.sum(exp_terms, axis=-1, keepdims=True)
    probability_low = probability.astype(bfloat)
    mixed_heads = jnp.einsum(
        "ngts,snd->tngd", probability_low, value_rows, preferred_element_type=single
    )
    attended = mixed_heads.reshape(TOK_DEV, HEADS * HEAD_DIM).astype(bfloat)
    branch = jnp.dot(attended, output_full, preferred_element_type=single)
    hidden = token_values + valid_rows * branch
    inv_second = rms_scale(hidden)
    normed_second = (hidden * inv_second * mix_gain_full).astype(bfloat)

    rows = jnp.concatenate(group_gather(normed_second), axis=0)
    logits = jnp.dot(rows, router_full, preferred_element_type=single)
    logits = jnp.where(pick_all, logits, -jnp.inf)
    terms = jnp.exp(logits - jnp.max(logits, axis=1, keepdims=True))
    combine = terms / jnp.sum(terms, axis=1, keepdims=True)
    lanes = expert_lanes().astype(bfloat)
    high = combine.astype(bfloat)
    low = (combine - high.astype(single)).astype(bfloat)
    combine_wide = jnp.dot(
        jnp.concatenate([high, low], axis=1), jnp.concatenate([lanes, lanes], axis=0),
        preferred_element_type=single,
    )
    acts = jnp.dot(rows, gate_up_full, preferred_element_type=single)
    gate_act, up_act = acts[:, :wide], acts[:, wide:]
    sigmoid_gate = jax.nn.sigmoid(gate_act)
    silu_gate = gate_act * sigmoid_gate
    inner_act = (silu_gate * up_act).astype(bfloat).astype(single)
    inner_scaled = (inner_act * combine_wide).astype(bfloat)
    mixture_part = jnp.dot(inner_scaled, down_full, preferred_element_type=single).astype(bfloat)
    grad_down = jnp.dot(grad_mixture, down_full.T, preferred_element_type=single)
    grad_gates = jnp.dot(
        inner_act * grad_down, lanes.T.astype(single), preferred_element_type=single,
        precision=lax.Precision.HIGH,
    )
    grad_logits = combine * (grad_gates - jnp.sum(combine * grad_gates, axis=1, keepdims=True))
    grad_logits = grad_logits.astype(bfloat)
    grad_inner = grad_down * combine_wide
    grad_acts = jnp.concatenate(
        [
            (grad_inner * up_act * sigmoid_gate * (1.0 + gate_act * (1.0 - sigmoid_gate))).astype(bfloat),
            (grad_inner * silu_gate).astype(bfloat),
        ],
        axis=1,
    )
    grad_rows = (
        jnp.dot(grad_acts, gate_up_full.T, preferred_element_type=single)
        + jnp.dot(grad_logits, router_full.T, preferred_element_type=single)
    ).astype(bfloat)
    blocks_of = lambda a: [a[i * TOK_DEV : (i + 1) * TOK_DEV] for i in range(8)]
    grad_normed_second = group_sum(blocks_of(grad_rows))
    mixture = group_sum(blocks_of(mixture_part))
    layer_out = (hidden + valid_rows * mixture).astype(bfloat)

    router_grad = jnp.dot(rows.T, grad_logits, preferred_element_type=single)
    gate_up_grad = jnp.dot(rows.T, grad_acts, preferred_element_type=single).astype(bfloat)
    down_grad = jnp.dot(inner_scaled.T, grad_mixture, preferred_element_type=single).astype(bfloat)
    gate_part = torus_sum(gate_up_grad[:, :wide].reshape(4, 4, 64, wide), "yx", "yx")
    up_part = torus_sum(gate_up_grad[:, wide:].reshape(4, 4, 64, wide), "xy", "yx")
    down_grad = down_grad.reshape(12, 16, 4, D).transpose(1, 0, 2, 3).reshape(4, 4, 48, D)
    down_owned = jnp.concatenate(
        [
            torus_sum(down_grad[..., : D // 2], "yx", "yx"),
            torus_sum(down_grad[..., D // 2 :], "xy", "yx"),
        ],
        axis=-1,
    ).reshape(12, 4, D)
    owned = jnp.stack([gate_part, up_part], axis=1).reshape(4, 2, 8, 2 * wide)
    owned = group_exchange(owned).reshape(8, 8, 24, 64).transpose(2, 1, 0, 3).reshape(24 * 8, FF)
    owned = jnp.dot(
        owned, order.T.astype(single), preferred_element_type=single, precision=lax.Precision.HIGHEST
    ).reshape(2, EXPERTS, 8, FF)
    gate_owned, up_owned = owned[0], owned[1]

    grad_hidden_norm, mixture_gain_grad = norm_backward(
        hidden, inv_second, mix_gain_full, grad_normed_second
    )
    grad_hidden = grad_out + grad_hidden_norm
    grad_branch = (valid_rows * grad_hidden).astype(bfloat)
    output_grad = jnp.dot(attended.T, grad_branch, preferred_element_type=single)
    grad_attended = (
        jnp.dot(grad_branch, output_full.T, preferred_element_type=single)
        .astype(bfloat)
        .reshape(TOK_DEV, KV_HEADS, group_size, HEAD_DIM)
    )
    grad_probability = jnp.einsum(
        "tngd,snd->ngts", grad_attended, value_rows, preferred_element_type=single
    )
    grad_values = (
        jnp.einsum("ngts,tngd->snd", probability_low, grad_attended, preferred_element_type=single)
        .astype(bfloat)
        .reshape(TOK_DEV, KV_HEADS * HEAD_DIM)
    )
    row_dot = jnp.sum(probability * grad_probability, axis=-1, keepdims=True)
    grad_scores = (probability * (grad_probability - row_dot)).astype(bfloat)
    grad_query_rot = (
        jnp.einsum("ngts,snd->tngd", grad_scores, key_rot, preferred_element_type=single)
        * score_scale
    )
    grad_key_rot = (
        jnp.einsum("ngts,tngd->snd", grad_scores, query_rot, preferred_element_type=single)
        * score_scale
    )
    grad_query = (
        rotate(grad_query_rot.reshape(TOK_DEV, HEADS, HEAD_DIM), cosine, -sine_part)
        .astype(bfloat)
        .reshape(TOK_DEV, HEADS * HEAD_DIM)
    )
    grad_key = (
        rotate(grad_key_rot, cosine, -sine_part)
        .astype(bfloat)
        .reshape(TOK_DEV, KV_HEADS * HEAD_DIM)
    )
    grad_qkv = jnp.concatenate([grad_query, grad_key, grad_values], axis=1)
    qkv_grad = jnp.dot(normed_first.T, grad_qkv, preferred_element_type=single)
    grad_normed_first = jnp.dot(grad_qkv, qkv_full.T, preferred_element_type=single)
    grad_tokens_norm, attention_gain_grad = norm_backward(
        token_values, inv_first, attn_gain_full, grad_normed_first
    )
    grad_tokens = (grad_hidden + grad_tokens_norm).astype(bfloat)

    small_grad = jnp.concatenate(
        [router_grad, attention_gain_grad[:, None], mixture_gain_grad[:, None], jnp.zeros((D, 114), single)],
        axis=1,
    )
    sums = []
    c = lax.axis_index("core")
    for part, turn in (
        (qkv_grad[:, :1024], "yxz"),
        (qkv_grad[:, 1024:], "xzy"),
        (jnp.concatenate([output_grad, small_grad], axis=1), "zyx"),
    ):
        part = part.reshape(4, 4, 4, 2, 8, -1)
        send = lax.dynamic_index_in_dim(part, 1 - c, 3, keepdims=False).astype(bfloat)
        keep = lax.dynamic_index_in_dim(part, c, 3, keepdims=False)
        both = (keep + shift(send, "core", 1).astype(single)).astype(bfloat)
        sums.append(torus_sum(both, turn, "yxz"))
    query_owned, key_value_owned, rest = sums
    return (
        layer_out,
        grad_tokens,
        query_owned,
        key_value_owned[:, :512],
        key_value_owned[:, 512:],
        rest[:, :1024],
        rest[:, 1036],
        rest[:, 1024:1036],
        rest[:, 1037],
        gate_owned,
        up_owned,
        down_owned,
    )


def solution(mesh):
    mesh = Mesh(mesh.devices.reshape(4, 4, 4, 2), ALL)
    rows, line, inner = P(ALL, None), P(ALL), P(None, ALL, None)
    return jax.shard_map(
        shards,
        mesh=mesh,
        in_specs=(rows,) * 8 + (line, rows, line) + (inner,) * 3,
        out_specs=(rows,) * 6 + (line, rows, line) + (inner,) * 3,
        check_vma=False,
    )
```

time: 1330 us -> 561 us (0.42)
  waiting for transfers between devices: 813 us -> 165 us
  starting transfers between devices: 0.25 us -> 133 us
  blocking collectives: 108 us -> 0 us
  local copies, waits for them, and re-layouts: 172 us -> 84.2 us
  matrix products: 178 us -> 108 us
    reduce_scatter x2 -> x0, waiting for transfers between devices: 496 us -> none  [the longest x1 251 us: shards(): lax.psum_scatter(up_grad, 'fsdp', scatter_dimension=1, tiled=True)]
    unnamed x7 -> x3, waiting for transfers between devices: 194 us -> 0.05 us
    ppermute x0 -> x111, starting transfers between devices: none -> 133 us  [shift(): return lax.ppermute(v, axis, [(i, (i + s) % n) for i in range(n)])]
    ppermute x0 -> x111, waiting for transfers between devices: none -> 98.4 us  [shift(): return lax.ppermute(v, axis, [(i, (i + s) % n) for i in range(n)])]
    dot_general x25 -> x19, matrix products: 168 us -> 95 us  [the longest x1 10 us: shards(): jnp.dot(grad_acts, gate_up_full.T, preferred_element_type=single)]
    unnamed x1 -> x0, blocking collectives: 70.4 us -> none
    all_gather x3, waiting for transfers between devices: 123 us -> 66.7 us  [the longest x1 28.8 us: shards(): lax.all_gather(jnp.concatenate([query_weight, key_weight, value_weight, o...]
    gather x4 -> x0, local copies, waits for them, and re-layouts: 54.9 us -> none  [the longest x1 15.7 us: shards(): pair_out = expert_out[destination].reshape(TOK_DEV, TOP, D)]
  transfers between devices with their start and end apart: 6 -> 114, of which waited for: 6 -> 39; matrix products, arithmetic and copies ran while one was open for 11% -> 27% of each run, Pallas kernels for 0% -> 0%
where the time goes in v1:
time: 561 us; the launch traced here: 554 us
  waiting for transfers between devices  165 us (29%)
  starting transfers between devices  133 us (24%)
  matrix products  108 us (19%)
  local copies, waits for them, and re-layouts  84.2 us (15%)
  other arithmetic  46.7 us (8%)
  between operations  16.6 us (3%)
    ppermute x111, starting transfers between devices, shift(): return lax.ppermute(v, axis, [(i, (i + s) % n) for i in range(n)])  133 us
    ppermute x111, waiting for transfers between devices, shift(): return lax.ppermute(v, axis, [(i, (i + s) % n) for i in range(n)])  98.4 us
    all_gather x1, waiting for transfers between devices, shards(): lax.all_gather(jnp.concatenate([query_weight, key_weight, value_weight, o...  28.8 us
    unnamed x170, local copies, waits for them, and re-layouts  20.1 us
    all_gather x1, waiting for transfers between devices, shards(): gate_up_full = lax.all_gather(gate_up, ('y', 'x'), axis=0, tiled=True)  19.9 us
    all_gather x1, waiting for transfers between devices, shards(): lax.all_gather(down_weight.reshape(48, D), ('y', 'x'), axis=0, tiled=True)  18 us
  transfers between devices with their start and end apart: 114, of which 39 were waited for; matrix products, arithmetic and copies ran while one was open for 27% of the time, Pallas kernels for 0%

profile of v1, /device:TPU:0, one launch (start us, length us, event | category | flops | bytes accessed | tf_op | source)
XLA Modules:
  0.0 553.6 jit_solution(16482663074145644427)
XLA Ops:
  13.8 4.2 collective-permute-start.13
  28.0 5.6 %collective-permute-done.9 = bf16[2,8,1536]{2,1,0:T(8,128)(2,1)S(1)} collective-permute-done((bf16[2,8,1536]{2,1,0:T(8,128)(2,1)S(1)}, bf16[2,8,1536]{2,1,0:T(8,128)(2,1)S(1)}, u32[]{:S(2)}, u32[]{:S(2)}) %collective-permute-start.9) | collective-permute-done | bytes 49184 | tf_op jit(solution)/shard_map/ppermute | solution.py:26
  34.7 4.7 collective-permute-done.11
  46.9 4.5 collective-permute-done.16
  55.0 28.8 %all-gather.4.cloned.1.call-done = bf16[1024,3200]{1,0:T(8,128)(2,1)} async-done(((bf16[8,3200]{1,0:T(8,128)(2,1)}), bf16[1024,3200]{1,0:T(8,128)(2,1)}) %all-gather.4.cloned.1.call-update) | async-done | bytes 6553616 | tf_op jit(solution)/shard_map/all_gather | solution.py:170
  109.7 18.0 %all-gather.8.cloned.1.call-done = bf16[768,1024]{1,0:T(8,128)(2,1)} async-done(((bf16[48,1024]{1,0:T(8,128)(2,1)}), bf16[768,1024]{1,0:T(8,128)(2,1)}) %all-gather.8.cloned.1.call-update) | async-done | bytes 1572880 | tf_op jit(solution)/shard_map/all_gather | solution.py:185
  141.6 8.8 %fusion.12 = f32[2048,768]{0,1:T(8,128)} fusion(bf16[768,1024]{1,0:T(8,128)(2,1)} %reshape.524, bf16[2048,1152]{0,1:T(8,128)(2,1)} %constant_dynamic-update-slice_fusion.17), kind=kOutput, calls=%fused_computation.25 | convolution fusion | flops 3221225472 | bytes 12058624 | tf_op jit(solution)/shard_map/dot_general | solution.py:251
  157.9 19.9 %all-gather.6.cloned.1.call-done = bf16[1024,1536]{1,0:T(8,128)(2,1)} async-done(((bf16[64,1536]{1,0:T(8,128)(2,1)}), bf16[1024,1536]{1,0:T(8,128)(2,1)}) %all-gather.6.cloned.1.call-update) | async-done | bytes 3145744 | tf_op jit(solution)/shard_map/all_gather | solution.py:184
  177.7 9.8 %fusion.262 = f32[2048,1536]{0,1:T(8,128)S(1)} fusion(bf16[2048,1024]{1,0:T(8,128)(2,1)} %constant_dynamic-update-slice_fusion, bf16[1024,1536]{1,0:T(8,128)(2,1)} %all-gather.6.cloned.1.call-done), kind=kOutput, calls=%fused_computation.620 | convolution fusion | flops 6442450944 | bytes 19922944 | tf_op jit(solution)/shard_map/dot_general | solution.py:244
  194.0 4.3 multiply_reduce_fusion.3
  198.4 8.3 %multiply_convert_fusion.1 = (bf16[2048,768]{0,1:T(8,128)(2,1)}, bf16[2048,768]{0,1:T(8,128)(2,1)}, f32[2048,768]{0,1:T(8,128)}) fusion(f32[2048,1536]{0,1:T(8,128)S(1)} %fusion.262, f32[2048,768]{0,1:T(8,128)} %fusion.12, pred[12,768]{1,0:T(8,128)(4,1)S(1)} %copy-done.40, bf16[2048,12]{0,1:T(8,128)(2,1)S(1)} %get-tuple-element.22, ...), kind=kOutput, calls=%fused_computation.8 | convolution fusion | flops 97732608 | bytes 31564800 | tf_op jit(solution)/shard_map/dot_general | solution.py:240
  206.7 8.9 %fusion.29 = bf16[768,1024]{1,0:T(8,128)(2,1)} fusion(bf16[2048,1152]{0,1:T(8,128)(2,1)} %constant_dynamic-update-slice_fusion.17, f32[2048,768]{0,1:T(8,128)} %get-tuple-element.195, bf16[2048,768]{0,1:T(8,128)(2,1)S(1)} %multiply_convert_fusion.2), kind=kOutput, calls=%fused_computation.58 | convolution fusion | flops 3226730496 | bytes 15204352 | tf_op jit(solution)/shard_map/dot_general | solution.py:277
  215.6 5.4 convolution_convert_fusion
  239.9 9.8 %fusion.9 = bf16[1024,1536]{1,0:T(8,128)(2,1)S(1)} fusion(bf16[2048,1024]{1,0:T(8,128)(2,1)} %constant_dynamic-update-slice_fusion, bf16[2048,768]{0,1:T(8,128)(2,1)} %get-tuple-element.27, bf16[2048,768]{0,1:T(8,128)(2,1)S(1)} %copy-done.67), kind=kOutput, calls=%fused_computation.21 | convolution fusion | flops 6456606720 | bytes 13631488 | tf_op jit(solution)/shard_map/dot_general | solution.py:276
  254.2 4.3 fusion.263
  258.4 10.0 %fusion.8 = f32[2048,1024]{1,0:T(8,128)S(1)} fusion(bf16[1024,1536]{1,0:T(8,128)(2,1)} %all-gather.6.cloned.1.call-done, bf16[2048,768]{0,1:T(8,128)(2,1)} %get-tuple-element.27, bf16[2048,768]{0,1:T(8,128)(2,1)} %get-tuple-element.26), kind=kOutput, calls=%fused_computation.20 | convolution fusion | flops 6455033856 | bytes 17825792 | tf_op jit(solution)/shard_map/dot_general | solution.py:267
  308.7 3.7 collective-permute-start.110
  383.0 15.7 %collective-permute-done.93 = f32[2,8,1536]{2,1,0:T(8,128)S(1)} collective-permute-done((f32[2,8,1536]{2,1,0:T(8,128)S(1)}, f32[2,8,1536]{2,1,0:T(8,128)S(1)}, u32[]{:S(2)}, u32[]{:S(2)}) %collective-permute-start.93) | collective-permute-done | bytes 98336 | tf_op jit(solution)/shard_map/ppermute | solution.py:26
  398.7 5.8 %collective-permute-done.94 = f32[2,8,1536]{2,1,0:T(8,128)S(1)} collective-permute-done((f32[2,8,1536]{2,1,0:T(8,128)S(1)}, f32[2,8,1536]{2,1,0:T(8,128)S(1)}, u32[]{:S(2)}, u32[]{:S(2)}) %collective-permute-start.94) | collective-permute-done | bytes 98336 | tf_op jit(solution)/shard_map/ppermute | solution.py:26
  409.1 10.6 %collective-permute-done.35 = bf16[256,1024]{1,0:T(8,128)(2,1)} collective-permute-done((bf16[256,1024]{1,0:T(8,128)(2,1)}, bf16[256,1024]{1,0:T(8,128)(2,1)}, u32[]{:S(2)}, u32[]{:S(2)}) %collective-permute-start.35) | collective-permute-done | bytes 524320 | tf_op jit(solution)/shard_map/ppermute | solution.py:26
  421.7 6.6 %collective-permute-done.27 = bf16[256,1024]{1,0:T(8,128)(2,1)S(1)} collective-permute-done((bf16[256,1024]{1,0:T(8,128)(2,1)S(1)}, bf16[256,1024]{1,0:T(8,128)(2,1)S(1)}, u32[]{:S(2)}, u32[]{:S(2)}) %collective-permute-start.27) | collective-permute-done | bytes 524320 | tf_op jit(solution)/shard_map/ppermute | solution.py:26
  441.5 4.8 fusion.75
  449.3 4.3 fusion.253
  459.3 6.2 %concatenate.223 = f32[4,4,4,2,8,1152]{5,4,3,2,1,0:T(8,128)} concatenate(f32[4,4,4,2,8,1024]{5,4,3,2,1,0:T(8,128)} %fusion.69, f32[4,4,4,2,8,12]{5,4,3,2,1,0:T(8,128)} %bitcast.653, f32[4,4,4,2,8,1]{5,4,3,2,1,0:T(8,128)S(1)} %concatenate.247, f32[4,4,4,2,8,1]{5,4,3,2,1,0:T(8,128)S(1)} %concatenate.248, f32[4,4,4,2,8,114]{5,4,3,2,1,0:T(8,128)S(1)} %broadcast_in_dim.50), dimensions={5} | concatenate | bytes 9437184 | tf_op jit(solution)/shard_map/concatenate | solution.py:351
  (623 shorter events, 324.0 us)
Async XLA Ops:
  7.2 76.6 %all-gather.4.cloned.1.call-start = ((), (), s32[]{:S(2)}) async-start(), calls=%async_computation | async-start | bytes 6604800 | tf_op jit(solution)/shard_map/all_gather | solution.py:170
  10.2 117.6 %all-gather.8.cloned.1.call-start = ((), (), s32[]{:S(2)}) async-start(), calls=%async_computation.2 | async-start | bytes 1671168 | tf_op jit(solution)/shard_map/all_gather | solution.py:185
  13.7 31.4 %collective-permute-start.12 = (bf16[256,1152]{0,1:T(8,128)(2,1)S(1)}, bf16[256,1152]{0,1:T(8,128)(2,1)S(1)}, u32[]{:S(2)}, u32[]{:S(2)}) collective-permute-start(bf16[256,1152]{0,1:T(8,128)(2,1)S(1)} %concatenate.194), channel_id=1, source_target_pairs={{0,1},{1,0},{2,3},{3,2},{4,5},{5,4},{6,7},{7,6},{8,9},{9,8},{10,11... | collective-permute-start | bytes 1769480 | tf_op jit(solution)/shard_map/ppermute | solution.py:26
  13.8 27.5 %collective-permute-start.13 = (bf16[256,1152]{0,1:T(8,128)(2,1)S(1)}, bf16[256,1152]{0,1:T(8,128)(2,1)S(1)}, u32[]{:S(2)}, u32[]{:S(2)}) collective-permute-start(bf16[256,1152]{0,1:T(8,128)(2,1)S(1)} %concatenate.194), channel_id=1, source_target_pairs={{0,6},{2,0},{4,2},{6,4},{1,7},{3,1},{5,3},{7,5},{8,14},{10,8},{12,... | collective-permute-start | bytes 1769480 | tf_op jit(solution)/shard_map/ppermute | solution.py:26
  21.3 156.4 %all-gather.6.cloned.1.call-start = ((), (), s32[]{:S(2)}) async-start(), calls=%async_computation.1 | async-start | bytes 3342336 | tf_op jit(solution)/shard_map/all_gather | solution.py:184
  44.5 63.2 %collective-permute-start.19 = (bf16[256,1152]{0,1:T(8,128)(2,1)}, bf16[256,1152]{0,1:T(8,128)(2,1)}, u32[]{:S(2)}, u32[]{:S(2)}) collective-permute-start(bf16[256,1152]{0,1:T(8,128)(2,1)} %collective-permute-done.15), channel_id=1, source_target_pairs={{0,1},{1,0},{2,3},{3,2},{4,5},{5,4},{6,7},{7,6},{8,9},{9,8},{10,11... | collective-permute-start | bytes 1769480 | tf_op jit(solution)/shard_map/ppermute | solution.py:26
  52.3 51.5 %collective-permute-start.18 = (bf16[256,1152]{0,1:T(8,128)(2,1)}, bf16[256,1152]{0,1:T(8,128)(2,1)}, u32[]{:S(2)}, u32[]{:S(2)}) collective-permute-start(bf16[256,1152]{0,1:T(8,128)(2,1)} %pad_maximum_fusion.6), channel_id=1, source_target_pairs={{0,1},{1,0},{2,3},{3,2},{4,5},{5,4},{6,7},{7,6},{8,9},{9,8},{10,11... | collective-permute-start | bytes 1769480 | tf_op jit(solution)/shard_map/ppermute | solution.py:26
  100.6 37.6 %collective-permute-start.3 = (bf16[256,1024]{1,0:T(8,128)(2,1)S(1)}, bf16[256,1024]{1,0:T(8,128)(2,1)S(1)}, u32[]{:S(2)}, u32[]{:S(2)}) collective-permute-start(bf16[256,1024]{1,0:T(8,128)(2,1)S(1)} %get-tuple-element.25), channel_id=1, source_target_pairs={{0,2},{2,4},{4,6},{6,0},{1,3},{3,5},{5,7},{7,1},{8,10},{10,12},{12... | collective-permute-start | bytes 1572872 | tf_op jit(solution)/shard_map/ppermute | solution.py:26
  100.6 39.2 %collective-permute-start.1 = (bf16[256,1024]{1,0:T(8,128)(2,1)S(1)}, bf16[256,1024]{1,0:T(8,128)(2,1)S(1)}, u32[]{:S(2)}, u32[]{:S(2)}) collective-permute-start(bf16[256,1024]{1,0:T(8,128)(2,1)S(1)} %get-tuple-element.25), channel_id=1, source_target_pairs={{0,6},{2,0},{4,2},{6,4},{1,7},{3,1},{5,3},{7,5},{8,14},{10,8},{12,... | collective-permute-start | bytes 1572872 | tf_op jit(solution)/shard_map/ppermute | solution.py:26
  233.2 39.2 %collective-permute-start.95 = (bf16[2,48,512]{2,1,0:T(8,128)(2,1)S(1)}, bf16[2,48,512]{2,1,0:T(8,128)(2,1)S(1)}, u32[]{:S(2)}, u32[]{:S(2)}) collective-permute-start(bf16[2,48,512]{2,1,0:T(8,128)(2,1)S(1)} %get-tuple-element.85), channel_id=1, source_target_pairs={{0,32},{32,64},{64,96},{96,0},{1,33},{33,65},{65,97},{97,1},{2,34}... | collective-permute-start | bytes 294920 | tf_op jit(solution)/shard_map/ppermute | solution.py:26
  234.0 39.2 %collective-permute-start.97 = (bf16[2,48,512]{2,1,0:T(8,128)(2,1)S(1)}, bf16[2,48,512]{2,1,0:T(8,128)(2,1)S(1)}, u32[]{:S(2)}, u32[]{:S(2)}) collective-permute-start(bf16[2,48,512]{2,1,0:T(8,128)(2,1)S(1)} %get-tuple-element.87), channel_id=1, source_target_pairs={{0,96},{32,0},{64,32},{96,64},{1,97},{33,1},{65,33},{97,65},{2,98}... | collective-permute-start | bytes 294920 | tf_op jit(solution)/shard_map/ppermute | solution.py:26
  236.5 36.7 %collective-permute-start.103 = (bf16[2,48,512]{2,1,0:T(8,128)(2,1)S(1)}, bf16[2,48,512]{2,1,0:T(8,128)(2,1)S(1)}, u32[]{:S(2)}, u32[]{:S(2)}) collective-permute-start(bf16[2,48,512]{2,1,0:T(8,128)(2,1)S(1)} %get-tuple-element.91), channel_id=1, source_target_pairs={{0,8},{8,16},{16,24},{24,0},{1,9},{9,17},{17,25},{25,1},{2,10},{10... | collective-permute-start | bytes 294920 | tf_op jit(solution)/shard_map/ppermute | solution.py:26
  237.3 39.3 %collective-permute-start.105 = (bf16[2,48,512]{2,1,0:T(8,128)(2,1)S(1)}, bf16[2,48,512]{2,1,0:T(8,128)(2,1)S(1)}, u32[]{:S(2)}, u32[]{:S(2)}) collective-permute-start(bf16[2,48,512]{2,1,0:T(8,128)(2,1)S(1)} %get-tuple-element.93), channel_id=1, source_target_pairs={{0,24},{8,0},{16,8},{24,16},{1,25},{9,1},{17,9},{25,17},{2,26},{10... | collective-permute-start | bytes 294920 | tf_op jit(solution)/shard_map/ppermute | solution.py:26
  250.0 26.7 %collective-permute-start.75 = (bf16[2,64,768]{2,1,0:T(8,128)(2,1)S(1)}, bf16[2,64,768]{2,1,0:T(8,128)(2,1)S(1)}, u32[]{:S(2)}, u32[]{:S(2)}) collective-permute-start(bf16[2,64,768]{2,1,0:T(8,128)(2,1)S(1)} %get-tuple-element.50), channel_id=1, source_target_pairs={{0,32},{32,64},{64,96},{96,0},{1,33},{33,65},{65,97},{97,1},{2,34}... | collective-permute-start | bytes 589832 | tf_op jit(solution)/shard_map/ppermute | solution.py:26
  276.6 37.9 %collective-permute-start.21 = (bf16[256,1024]{1,0:T(8,128)(2,1)S(1)}, bf16[256,1024]{1,0:T(8,128)(2,1)S(1)}, u32[]{:S(2)}, u32[]{:S(2)}) collective-permute-start(bf16[256,1024]{1,0:T(8,128)(2,1)S(1)} %get-tuple-element.40), channel_id=1, source_target_pairs={{0,1},{1,0},{2,3},{3,2},{4,5},{5,4},{6,7},{7,6},{8,9},{9,8},{10,11... | collective-permute-start | bytes 1572872 | tf_op jit(solution)/shard_map/ppermute | solution.py:26
  276.7 38.7 %collective-permute-start.22 = (bf16[256,1024]{1,0:T(8,128)(2,1)}, bf16[256,1024]{1,0:T(8,128)(2,1)S(1)}, u32[]{:S(2)}, u32[]{:S(2)}) collective-permute-start(bf16[256,1024]{1,0:T(8,128)(2,1)} %get-tuple-element.39), channel_id=1, source_target_pairs={{0,1},{1,0},{2,3},{3,2},{4,5},{5,4},{6,7},{7,6},{8,9},{9,8},{10,11... | collective-permute-start | bytes 1572872 | tf_op jit(solution)/shard_map/ppermute | solution.py:26
  278.1 37.8 %collective-permute-start.25 = (bf16[256,1024]{1,0:T(8,128)(2,1)}, bf16[256,1024]{1,0:T(8,128)(2,1)}, u32[]{:S(2)}, u32[]{:S(2)}) collective-permute-start(bf16[256,1024]{1,0:T(8,128)(2,1)} %get-tuple-element.38), channel_id=1, source_target_pairs={{0,1},{1,0},{2,3},{3,2},{4,5},{5,4},{6,7},{7,6},{8,9},{9,8},{10,11... | collective-permute-start | bytes 1572872 | tf_op jit(solution)/shard_map/ppermute | solution.py:26
  315.4 106.3 %collective-permute-start.20 = (bf16[256,1024]{1,0:T(8,128)(2,1)}, bf16[256,1024]{1,0:T(8,128)(2,1)}, u32[]{:S(2)}, u32[]{:S(2)}) collective-permute-start(bf16[256,1024]{1,0:T(8,128)(2,1)} %get-tuple-element.37), channel_id=1, source_target_pairs={{0,1},{1,0},{2,3},{3,2},{4,5},{5,4},{6,7},{7,6},{8,9},{9,8},{10,11... | collective-permute-start | bytes 1572872 | tf_op jit(solution)/shard_map/ppermute | solution.py:26
  332.6 75.6 %collective-permute-start.28 = (bf16[256,1024]{1,0:T(8,128)(2,1)}, bf16[256,1024]{1,0:T(8,128)(2,1)}, u32[]{:S(2)}, u32[]{:S(2)}) collective-permute-start(bf16[256,1024]{1,0:T(8,128)(2,1)} %get-tuple-element.30), channel_id=1, source_target_pairs={{0,1},{1,0},{2,3},{3,2},{4,5},{5,4},{6,7},{7,6},{8,9},{9,8},{10,11... | collective-permute-start | bytes 1572872 | tf_op jit(solution)/shard_map/ppermute | solution.py:26
  332.6 29.8 %collective-permute-start.23 = (bf16[128,1024]{1,0:T(8,128)(2,1)}, bf16[128,1024]{1,0:T(8,128)(2,1)}, u32[]{:S(2)}, u32[]{:S(2)}) collective-permute-start(bf16[128,1024]{1,0:T(8,128)(2,1)} %get-tuple-element.102), channel_id=1, source_target_pairs={{0,2},{2,4},{4,6},{6,0},{1,3},{3,5},{5,7},{7,1},{8,10},{10,12},{12... | collective-permute-start | bytes 786440 | tf_op jit(solution)/shard_map/ppermute | solution.py:26
  369.3 52.5 %collective-permute-start.24 = (bf16[256,1024]{1,0:T(8,128)(2,1)}, bf16[256,1024]{1,0:T(8,128)(2,1)}, u32[]{:S(2)}, u32[]{:S(2)}) collective-permute-start(bf16[256,1024]{1,0:T(8,128)(2,1)} %pad_maximum_fusion.9), channel_id=1, source_target_pairs={{0,2},{2,4},{4,6},{6,0},{1,3},{3,5},{5,7},{7,1},{8,10},{10,12},{12... | collective-permute-start | bytes 1572872 | tf_op jit(solution)/shard_map/ppermute | solution.py:26
  373.3 35.8 %collective-permute-start.32 = (bf16[256,1024]{1,0:T(8,128)(2,1)}, bf16[256,1024]{1,0:T(8,128)(2,1)}, u32[]{:S(2)}, u32[]{:S(2)}) collective-permute-start(bf16[256,1024]{1,0:T(8,128)(2,1)} %pad_maximum_fusion.11), channel_id=1, source_target_pairs={{0,2},{2,4},{4,6},{6,0},{1,3},{3,5},{5,7},{7,1},{8,10},{10,12},{12... | collective-permute-start | bytes 1572872 | tf_op jit(solution)/shard_map/ppermute | solution.py:26
  492.1 28.1 %collective-permute-start.64 = (bf16[4,4,8,1152]{3,2,1,0:T(8,128)(2,1)S(1)}, bf16[4,4,8,1152]{3,2,1,0:T(8,128)(2,1)S(1)}, u32[]{:S(2)}, u32[]{:S(2)}) collective-permute-start(bf16[4,4,8,1152]{3,2,1,0:T(8,128)(2,1)S(1)} %pad_maximum_fusion.21), channel_id=1, source_target_pairs={{0,2},{2,4},{4,6},{6,0},{1,3},{3,5},{5,7},{7,1},{8,10},{10,12},{12... | collective-permute-start | bytes 884744 | tf_op jit(solution)/shard_map/ppermute | solution.py:26
  493.4 26.9 %collective-permute-start.66 = (bf16[4,4,8,1152]{3,2,1,0:T(8,128)(2,1)S(1)}, bf16[4,4,8,1152]{3,2,1,0:T(8,128)(2,1)S(1)}, u32[]{:S(2)}, u32[]{:S(2)}) collective-permute-start(bf16[4,4,8,1152]{3,2,1,0:T(8,128)(2,1)S(1)} %pad_maximum_fusion.22), channel_id=1, source_target_pairs={{0,6},{2,0},{4,2},{6,4},{1,7},{3,1},{5,3},{7,5},{8,14},{10,8},{12,... | collective-permute-start | bytes 884744 | tf_op jit(solution)/shard_map/ppermute | solution.py:26
  (162 other events, 1636.8 us)
Sparse Core Ops, SparseCore 0:
  11.6 72.2 all-gather.3
  86.5 41.2 all-gather.7
  130.5 47.2 all-gather.5
